TPU v7x, 256 devices: a whole 4x4x8 slice. The times are simulated.
256 devices in a mesh: seq: 32 (over y, x, core), dp: 8 (over z).
Axes of the slice: x: 4, y: 4, z: 8, core: 2. Of those that a mesh axis runs over, the one named last changes fastest.
Arguments:
- queries: bfloat16 [16384, 4096], P('seq', 'dp'), may hold values from -6 to 6
- keys: bfloat16 [16384, 4096], P('seq', 'dp'), may hold values from -6 to 6
- values: bfloat16 [16384, 4096], P('seq', 'dp'), may hold values from -102 to 102
- out_grad: bfloat16 [16384, 4096], P('seq'), may hold values from -6 to 6
- gain: bfloat16 [32, 128], P('dp', 'seq'), may hold values from 0.099609375 to 1.8984375
- out_weight: bfloat16 [4096, 4096], P('dp', 'seq'), may hold values from -0.09375 to 0.09375
Outputs:
- query_grad: bfloat16 [16384, 4096], P('seq', 'dp')
- key_grad: bfloat16 [16384, 4096], P('seq', 'dp')
- value_grad: bfloat16 [16384, 4096], P('seq', 'dp')
- weight_grad: float32 [4096, 4096], P('dp', 'seq')
- gain_grad: float32 [32, 128], P('dp', 'seq')
All inputs are finite; a program needn't handle non-finite values.
Results may differ from a plain program's by a relative error of at most 0.006.
Values may be sent and summed in bfloat16 or wider, within the bound.
A program may use at most 128 MiB of HBM per device.

v0:
```python
import jax
import jax.numpy as jnp
from jax import lax
from jax.sharding import PartitionSpec as P

HD = 128
BLK = 512
D = 4096


EPSILON = 1e-06


def prefix(value, axis, join, neutral, backward):
    count, mine = (lax.axis_size(axis), lax.axis_index(axis))
    pieces = lax.all_gather(value, axis)
    if backward:
        pieces = pieces[::-1]
        mine = count - 1 - mine
    so_far = jnp.full_like(value, 0) + jnp.asarray(neutral, value.dtype)

    def step(position, so_far):
        longer = join(so_far, pieces[position])
        return jnp.where(position < mine, longer, so_far)

    return lax.fori_loop(0, count - 1, step, so_far)


def causal_mask(size):
    rows = lax.broadcasted_iota(jnp.int32, (size, size), 0)
    cols = lax.broadcasted_iota(jnp.int32, (size, size), 1)
    return (cols <= rows).astype(jnp.float32)


def add_states(earlier, later):
    return earlier + later


def body(queries, keys, values, out_grad, gain, out_weight):
    rows, width = queries.shape
    heads = width // HD
    count = rows // BLK
    lower = causal_mask(BLK)
    weight_rows, gain_rows = (
        lax.all_gather(out_weight, "seq", axis=1, tiled=True),
        lax.all_gather(gain, "seq", axis=1, tiled=True),
    )
    query_blocks = queries.reshape(count, BLK, heads, HD)
    key_blocks = keys.reshape(count, BLK, heads, HD)
    value_blocks = values.reshape(count, BLK, heads, HD)
    kv_blocks = jnp.einsum(
        "nthi,nthj->nhij", key_blocks, value_blocks, preferred_element_type=jnp.float32
    )
    kv_device = jnp.sum(kv_blocks, axis=0)
    zero_state = jnp.zeros((heads, HD, HD), jnp.float32)
    state_device = prefix(kv_device, "seq", add_states, zero_state, False)
    running = jnp.cumsum(kv_blocks, axis=0)
    before = jnp.concatenate([jnp.zeros_like(kv_blocks), running[:-1]], axis=0)
    state_in = (state_device[None] + before).astype(jnp.bfloat16)
    scores = jnp.einsum(
        "nthi,nuhi->nhtu", query_blocks, key_blocks, preferred_element_type=jnp.float32
    )
    scores = (scores * lower).astype(jnp.bfloat16)
    attended = jnp.einsum(
        "nhtu,nuhj->nthj", scores, value_blocks, preferred_element_type=jnp.float32
    )
    attended = attended + jnp.einsum(
        "nthi,nhij->nthj", query_blocks, state_in, preferred_element_type=jnp.float32
    )
    attended = attended.reshape(rows, width)
    gain_flat = gain_rows.reshape(width).astype(jnp.float32)
    upstream = jnp.einsum("tc,fc->tf", out_grad, weight_rows, preferred_element_type=jnp.float32)
    weighted = upstream * gain_flat
    squares_local = jnp.sum(attended * attended, axis=1)
    inner_local = jnp.sum(weighted * attended, axis=1)
    squares = lax.psum(squares_local, "dp")
    inner = lax.psum(inner_local, "dp")
    inv_rms = lax.rsqrt(squares / D + EPSILON)
    normed = (attended * inv_rms[:, None] * gain_flat).astype(jnp.bfloat16)
    p_grad = (inv_rms[:, None] * weighted - attended * (inv_rms**3 * inner / D)[:, None]).astype(
        jnp.bfloat16
    )
    weight_term = jnp.einsum("tf,tc->fc", normed, out_grad, preferred_element_type=jnp.float32)
    gain_term = jnp.sum(upstream * attended * inv_rms[:, None], axis=0).reshape(heads, HD)
    weight_grad, gain_grad = (
        lax.psum_scatter(weight_term, "seq", scatter_dimension=1, tiled=True),
        lax.psum_scatter(gain_term, "seq", scatter_dimension=1, tiled=True),
    )
    grad_blocks = p_grad.reshape(count, BLK, heads, HD)
    qg_blocks = jnp.einsum(
        "nthi,nthj->nhij", query_blocks, grad_blocks, preferred_element_type=jnp.float32
    )
    qg_device = jnp.sum(qg_blocks, axis=0)
    later_device = prefix(qg_device, "seq", add_states, zero_state, True)
    flipped = jnp.cumsum(qg_blocks[::-1], axis=0)
    after = jnp.concatenate([jnp.zeros_like(qg_blocks), flipped[:-1]], axis=0)[::-1]
    later_in = (later_device[None] + after).astype(jnp.bfloat16)
    back = jnp.einsum(
        "nthj,nuhj->nhtu", grad_blocks, value_blocks, preferred_element_type=jnp.float32
    )
    back = (back * lower).astype(jnp.bfloat16)
    query_grad = jnp.einsum("nhtu,nuhi->nthi", back, key_blocks, preferred_element_type=jnp.float32)
    query_grad = query_grad + jnp.einsum(
        "nthj,nhij->nthi", grad_blocks, state_in, preferred_element_type=jnp.float32
    )
    key_grad = jnp.einsum("nhtu,nthi->nuhi", back, query_blocks, preferred_element_type=jnp.float32)
    key_grad = key_grad + jnp.einsum(
        "nuhj,nhij->nuhi", value_blocks, later_in, preferred_element_type=jnp.float32
    )
    value_grad = jnp.einsum(
        "nhtu,nthj->nuhj", scores, grad_blocks, preferred_element_type=jnp.float32
    )
    value_grad = value_grad + jnp.einsum(
        "nuhi,nhij->nuhj", key_blocks, later_in, preferred_element_type=jnp.float32
    )
    return (
        query_grad.reshape(rows, width).astype(jnp.bfloat16),
        key_grad.reshape(rows, width).astype(jnp.bfloat16),
        value_grad.reshape(rows, width).astype(jnp.bfloat16),
        weight_grad,
        gain_grad,
    )


def solution(mesh):
    return jax.shard_map(
        body,
        mesh=mesh,
        in_specs=(
            P("seq", "dp"),
            P("seq", "dp"),
            P("seq", "dp"),
            P("seq", None),
            P("dp", "seq"),
            P("dp", "seq"),
        ),
        out_specs=(P("seq", "dp"), P("seq", "dp"), P("seq", "dp"), P("dp", "seq"), P("dp", "seq")),
        check_vma=False,
    )
```

profile of v0, /device:TPU:1, one launch (start us, length us, event | category | flops | bytes accessed | tf_op | source)
XLA Modules:
  0.0 321.4 jit_solution(70350550315464211)
XLA Ops:
  7.2 1.3 copy.124
  8.6 2.2 fusion.15
  11.7 1.1 fusion.11
  13.5 25.8 %all-gather.2 = bf16[32,4,4]{2,1,0:T(4,128)(2,1)S(1)} all-gather(bf16[1,4,4]{2,1,0:T(4,128)(2,1)S(1)} %bitcast.158), channel_id=1, replica_groups=mesh['seq'=32,'dp'=8] {'seq'}, dimensions={0}, use_global_device_ids=true | all-gather | bytes 1056 | tf_op jit(solution)/shard_map/all_gather | solution.py:46
  39.4 2.1 multiply_convert_fusion.1
  41.5 1.8 convolution_bitcast_fusion.2
  43.3 30.0 %all-gather.9.cloned.1.call-done = f32[128,128,128]{2,1,0:T(8,128)} async-done(((f32[4,128,128]{2,1,0:T(8,128)}), f32[128,128,128]{2,1,0:T(8,128)}) %all-gather.9.cloned.1.call-update) | async-done | bytes 8388624 | tf_op jit(solution)/shard_map/all_gather | solution.py:16
  73.3 33.0 %while.28 = (s32[]{:T(128)}, f32[4,128,128]{2,1,0:T(8,128)S(1)}, s32[]{:T(128)}, f32[32,4,128,128]{3,2,1,0:T(8,128)}, s32[]{:T(128)}, /*index=5*/s32[]{:T(128)}) while((s32[]{:T(128)}, f32[4,128,128]{2,1,0:T(8,128)S(1)}, s32[]{:T(128)}, f32[32,4,128,128]{3,2,1,0:T(8,128)}, s32[]{:T(128)}, /*index=5*/s32[]{:T(128)}) %tuple.84), condition=%wide.region_1.2_spmd.clone, body=%wide.region_0.0_spmd.clone.sunk | while | flops 196612 | bytes 786533 | solution.py:26
  106.3 2.6 fusion.10
  109.0 14.1 %psum.14 = f32[512]{0:T(512)S(1)} all-reduce(f32[512]{0:T(512)S(1)} %get-tuple-element.229), channel_id=1, replica_groups=mesh['seq'=32,'dp'=8] {'dp'}, use_global_device_ids=true, to_apply=%region_3.4 | all-reduce | flops 512 | bytes 4096 | tf_op jit(solution)/shard_map/psum | solution.py:76
  123.1 6.6 %all-gather.7.cloned.1.call-done = bf16[512,4096]{1,0:T(8,128)(2,1)} async-done(((bf16[512,128]{1,0:T(8,128)(2,1)}), bf16[512,4096]{1,0:T(8,128)(2,1)}) %all-gather.7.cloned.1.call-update) | async-done | bytes 4194320 | tf_op jit(solution)/shard_map/all_gather | solution.py:45
  129.7 7.3 %fusion.9 = (f32[512]{0:T(512)S(1)}, f32[512]{0:T(512)S(1)}, bf16[512,512]{0,1:T(8,128)(2,1)}, f32[512,512]{0,1:T(8,128)}) fusion(f32[4,128,512]{2,1,0:T(8,128)} %get-tuple-element.230, f32[512]{0:T(512)S(1)} %add_rsqrt_fusion, f32[512]{0:T(512)S(1)} %bitcast.156, bf16[512,4096]{1,0:T(8,128)(2,1)} %param.13, bf16[512,4096]{1,0:T(8,128)(2,1)} %all-gather.7.cloned.1.call-done), kind=kOutput, calls=%fused_computation.25 | convolution fusion | flops 2149841920 | bytes 11018240 | tf_op jit(solution)/shard_map/tc,fc->tf/dot_general | solution.py:72
  137.0 13.9 %psum.15 = f32[512]{0:T(512)S(1)} all-reduce(f32[512]{0:T(512)S(1)} %get-tuple-element.211), channel_id=1, replica_groups=mesh['seq'=32,'dp'=8] {'dp'}, use_global_device_ids=true, to_apply=%region_5.6 | all-reduce | flops 512 | bytes 4096 | tf_op jit(solution)/shard_map/psum | solution.py:77
  150.9 1.7 fusion.5
  153.9 7.9 %fusion.40 = f32[512,4096]{1,0:T(8,128)} fusion(bf16[512,512]{0,1:T(8,128)(2,1)} %get-tuple-element.228, bf16[512,4096]{1,0:T(8,128)(2,1)} %param.13), kind=kOutput, calls=%fused_computation.61 | convolution fusion | flops 2147483648 | bytes 13107200 | tf_op jit(solution)/shard_map/tf,tc->fc/dot_general | solution.py:83
  163.7 2.2 multiply_convert_fusion
  166.0 1.3 copy-done.1
  168.1 1.1 fusion
  169.2 2.0 copy.73
  171.2 66.7 %all-reduce = f32[4,128]{1,0:T(4,128)S(1)} all-reduce(f32[4,128]{1,0:T(4,128)S(1)} %bitcast.159), channel_id=5, replica_groups=mesh['seq'=32,'dp'=8] {'seq'}, use_global_device_ids=true, to_apply=%region_10.11.clone | all-reduce | flops 512 | bytes 4096
  238.6 1.5 fusion.39
  240.6 8.2 %rev.3 = f32[32,4,128,128]{3,2,1,0:T(8,128)} reverse(f32[32,4,128,128]{3,2,1,0:T(8,128)} %bitcast.148), dimensions={0} | reverse | bytes 16777216 | tf_op jit(solution)/shard_map/rev | solution.py:18
  248.8 33.3 %while.29 = (s32[]{:T(128)}, f32[4,128,128]{2,1,0:T(8,128)S(1)}, s32[]{:T(128)}, f32[32,4,128,128]{3,2,1,0:T(8,128)}, s32[]{:T(128)}, /*index=5*/s32[]{:T(128)}) while((s32[]{:T(128)}, f32[4,128,128]{2,1,0:T(8,128)S(1)}, s32[]{:T(128)}, f32[32,4,128,128]{3,2,1,0:T(8,128)}, s32[]{:T(128)}, /*index=5*/s32[]{:T(128)}) %tuple.73), condition=%wide.region_7.8_spmd.clone, body=%wide.region_6.7_spmd.clone.sunk | while | flops 196612 | bytes 786533 | solution.py:26
  248.8 1.1 add_select_fusion.5
  251.0 1.1 add_select_fusion.5
  255.3 1.1 add_select_fusion.5
  256.4 1.1 add_select_fusion.5
  271.4 1.1 add_select_fusion.5
  276.8 1.1 add_select_fusion.5
  281.1 1.1 add_select_fusion.5
  282.1 1.6 fusion.2
  286.1 28.8 %reduce-scatter.3.cloned.1.call-done = f32[512,128]{1,0:T(8,128)} async-done(((f32[512,4096]{1,0:T(8,128)}), f32[512,128]{1,0:T(8,128)}) %reduce-scatter.3.cloned.1.call-update) | async-done | bytes 262160 | tf_op jit(solution)/shard_map/reduce_scatter | solution.py:86
  (100 shorter events, 65.8 us)
Async XLA Ops:
  7.2 32.2 %copy-start = (bf16[512,512]{1,0:T(8,128)(2,1)S(1)}, bf16[512,512]{1,0:T(8,128)(2,1)}, u32[]{:S(2)}) copy-start(bf16[512,512]{1,0:T(8,128)(2,1)} %param.10) | copy-start | bytes 1572868
  7.2 34.3 %copy-start.5 = (bf16[512,512]{1,0:T(8,128)(2,1)S(1)}, bf16[512,512]{1,0:T(8,128)(2,1)}, u32[]{:S(2)}) copy-start(bf16[512,512]{1,0:T(8,128)(2,1)} %param.12) | copy-start | bytes 1572868
  7.2 66.1 %all-gather.9.cloned.1.call-start = ((), (), s32[]{:S(2)}) async-start(), calls=%async_computation.3 | async-start | bytes 8650752 | tf_op jit(solution)/shard_map/all_gather | solution.py:16
  8.6 30.7 %copy-start.7 = (bf16[512,512]{0,1:T(8,128)(2,1)}, bf16[512,512]{0,1:T(8,128)(2,1)S(1)}, u32[]{:S(2)}) copy-start(bf16[512,512]{0,1:T(8,128)(2,1)S(1)} %copy.124) | copy-start | bytes 1572868
  10.8 118.9 %all-gather.7.cloned.1.call-start = ((), (), s32[]{:S(2)}) async-start(), calls=%async_computation.1 | async-start | bytes 4325376 | tf_op jit(solution)/shard_map/all_gather | solution.py:45
  11.6 229.0 %all-gather.11.cloned.1.call-start = ((), (), s32[]{:S(2)}) async-start(), calls=%async_computation.4 | async-start | bytes 8650752 | tf_op jit(solution)/shard_map/all_gather | solution.py:16
  106.3 30.7 %copy-start.3 = (f32[4,128,128]{2,1,0:T(8,128)}, f32[4,128,128]{2,1,0:T(8,128)S(1)}, u32[]{:S(2)}) copy-start(f32[4,128,128]{2,1,0:T(8,128)S(1)} %get-tuple-element.163) | copy-start | bytes 786436
  153.8 161.0 %reduce-scatter.3.cloned.1.call-start = ((), (), s32[]{:S(2)}) async-start(), calls=%async_computation.2 | async-start | bytes 8650752 | tf_op jit(solution)/shard_map/reduce_scatter | solution.py:86
  161.8 0.7 copy-start.10
  163.7 3.6 %copy-start.8 = (bf16[512,512]{0,1:T(8,128)(2,1)S(1)}, bf16[512,512]{0,1:T(8,128)(2,1)}, u32[]{:S(2)}) copy-start(bf16[512,512]{0,1:T(8,128)(2,1)} %copy-done.7) | copy-start | bytes 1572868
  163.7 4.4 %copy-start.4 = (f32[4,128,128]{2,1,0:T(8,128)S(1)}, f32[4,128,128]{2,1,0:T(8,128)}, u32[]{:S(2)}) copy-start(f32[4,128,128]{2,1,0:T(8,128)} %copy-done.3) | copy-start | bytes 786436
  165.9 1.4 copy-start.1
  237.9 2.1 copy-start.2
  240.6 41.5 %copy-start.9 = (bf16[512,512]{1,0:T(8,128)(2,1)S(1)}, bf16[512,512]{1,0:T(8,128)(2,1)}, u32[]{:S(2)}) copy-start(bf16[512,512]{1,0:T(8,128)(2,1)} %param.11) | copy-start | bytes 1572868
  248.8 35.9 %copy-start.6 = (bf16[512,512]{1,0:T(8,128)(2,1)S(1)}, bf16[512,512]{1,0:T(8,128)(2,1)}, u32[]{:S(2)}) copy-start(bf16[512,512]{1,0:T(8,128)(2,1)} %param.12) | copy-start | bytes 1572868
Sparse Core Ops, SparseCore 0:
  11.2 62.1 all-gather.8
  75.8 53.8 all-gather.6
  153.9 58.6 all-gather.10
  217.0 97.7 reduce-scatter.2
where the time goes:
time: 324 us; the launch traced here: 321 us
  blocking collectives  120 us (37%)
  other arithmetic  67.7 us (21%)
  waiting for transfers between devices  66.2 us (20%)
  matrix products  32.3 us (10%)
  local copies, waits for them, and re-layouts  18.6 us (6%)
  between operations  14.6 us (5%)
    unnamed x1, blocking collectives  66.7 us
    select_n x62, other arithmetic, step(): return jnp.where(position < mine, longer, so_far)  64.8 us
    all_gather x2, waiting for transfers between devices, prefix(): pieces = lax.all_gather(value, axis)  30.1 us
    reduce_scatter x1, waiting for transfers between devices, body(): lax.psum_scatter(weight_term, 'seq', scatter_dimension=1, tiled=True)  28.8 us
    all_gather x1, blocking collectives, body(): lax.all_gather(gain, 'seq', axis=1, tiled=True)  25.8 us
    psum x1, blocking collectives, body(): squares = lax.psum(squares_local, 'dp')  14.1 us
    psum x1, blocking collectives, body(): inner = lax.psum(inner_local, 'dp')  13.9 us
    rev x1, local copies, waits for them, and re-layouts, prefix(): pieces = pieces[::-1]  8.23 us
  transfers between devices with their start and end apart: 4, of which 3 were waited for; matrix products, arithmetic and copies ran while one was open for 32% of the time, Pallas kernels for 0%

commit v1 on v0

v1 whole, which is shorter than its diff:
```python
import jax
import jax.numpy as jnp
from jax import lax
from jax.experimental import pallas as pl
from jax.experimental.pallas import tpu as pltpu
from jax.sharding import PartitionSpec as P

HD = 128
TOK = 512
WID = 512
NH = 4
D = 4096
EPSILON = 1e-06
HALF = 256
BF = jnp.bfloat16
F32 = jnp.float32
MESH = pl.DeviceIdType.MESH
STEPS = (0, 3, 1, 2)
ORDER = (2, 1, 3, 0)


def nt(a, b):
    return lax.dot_general(a, b, (((1,), (1,)), ((), ())), preferred_element_type=F32)


def tn(a, b):
    return lax.dot_general(a, b, (((0,), (0,)), ((), ())), preferred_element_type=F32)


def nn(a, b):
    return jnp.dot(a, b, preferred_element_type=F32)


def layer_kernel(
    q_hbm, k_hbm, v_hbm, og_hbm, gain_ref, w_hbm,
    dq_hbm, dk_hbm, dv_hbm, wg_hbm, gg_ref,
    q, k, v, og, wall, scores_t, q_t, att, up, p, n_t, dkp, dvp, dq_o, dk_o, dv_o, wg_o,
    kvs, s0s, s0r, s1s, s1r, s2s, s2r, fin, st, zb, gflat, col,
    sib_out, sib_in, part, ra, pb_buf, rb,
    load_sem, out_sem, ag_send, ag_recv, ag_sib, sc_send, sc_recv, z_send, z_recv,
    rs_send, rs_recv, rsb_recv, pair_send, pair_recv,
):
    s = lax.axis_index("seq")
    z = lax.axis_index("dp")
    y, x, c = s // 8, (s // 2) % 4, s % 2
    o = 1 - c
    pa, pb = x + c * (y - x), y + c * (x - y)

    def chip(da, db):
        a, b = (pa + da) % 4, (pb + db) % 4
        return a * (1 + 3 * c) + b * (4 - 3 * c)

    def chip_o(da, db):
        a, b = (pb + da) % 4, (pa + db) % 4
        return a * (1 + 3 * o) + b * (4 - 3 * o)

    def dev(da, db):
        return (2 * chip(da, db) + c, z)

    sib = (s + 1 - 2 * c, z)

    loads = [
        pltpu.make_async_copy(src, dst, load_sem.at[i])
        for i, (src, dst) in enumerate(
            [(k_hbm, k), (v_hbm, v), (w_hbm, wall.at[s]), (q_hbm, q), (og_hbm, og)]
        )
    ]
    for load in loads:
        load.start()

    barrier = pltpu.get_barrier_semaphore()
    partners = [dev(i, 0) for i in (1, 2, 3)] + [dev(0, i) for i in (1, 2, 3)] + [sib]
    partners += [(s, (z + i) % 8) for i in range(1, 8)]
    for d in partners:
        pl.semaphore_signal(barrier, inc=1, device_id=d, device_id_type=MESH)

    def send(src, dst, ssem, rsem, d):
        pltpu.make_async_remote_copy(
            src_ref=src, dst_ref=dst, send_sem=ssem, recv_sem=rsem,
            device_id=d, device_id_type=MESH,
        ).start()

    def await_(ref, sem):
        pltpu.make_async_copy(ref, ref, sem).wait()

    def head(h):
        return pl.ds(pl.multiple_of(h * HD, HD), HD)

    def rows(h, n=HD):
        return pl.ds(pl.multiple_of(h * n, n), n)

    lane = lax.broadcasted_iota(jnp.int32, (HD, HD), 1)
    subl = lax.broadcasted_iota(jnp.int32, (HD, HD), 0)
    eye = lane == subl

    def to_rows(column):
        return jnp.sum(jnp.where(eye, column, 0.0), axis=0, keepdims=True)

    def to_column(row):
        return jnp.sum(jnp.where(eye, row, 0.0), axis=1, keepdims=True)

    def two(rows4):
        high = rows4.astype(BF).astype(F32)
        return jnp.concatenate([high, rows4 - high, jnp.zeros((8, HD), F32)], axis=0)

    def one(rows16):
        return rows16[:NH] + rows16[NH:2 * NH]

    def before(i, j, backward):
        return (i > j) if backward else (i < j)

    own_half = rows(c, HALF)

    def scan_start(n, extra):
        s0s[n, 0:HALF, :] = kvs[n, rows(o, HALF), :]
        s0s[n, HALF:, :] = extra
        send(s0s.at[n], s0r.at[n], sc_send.at[n, 0], sc_recv.at[n, 0], sib)

    def scan_ring_a(n, extra):
        await_(s0r.at[n], sc_recv.at[n, 0])
        s1s[n, 0:HALF, :] = (kvs[n, own_half, :] + s0r[n, 0:HALF, :]).astype(BF)
        s1s[n, HALF:, :] = two(one(extra + s0r[n, HALF:, :])).astype(BF)
        for i in (1, 2, 3):
            send(s1s.at[n], s1r.at[n, i - 1], sc_send.at[n, 1], sc_recv.at[n, i], dev(i, 0))

    def scan_ring_b(n, backward):
        for i in (1, 2, 3):
            await_(s1r.at[n, i - 1], sc_recv.at[n, i])
        mine = s1s[n].astype(F32)
        lower, total = jnp.zeros_like(mine), mine
        for i in (1, 2, 3):
            got = s1r[n, i - 1].astype(F32)
            flag = before((pa - i + 4) % 4, pa, backward)
            lower = lower + jnp.where(flag, got, 0.0)
            total = total + got
        first = c == 0
        low = jnp.where(first, total, lower)
        high = jnp.where(first, total, lower + mine)
        s2s[n, 0, 0:HALF, :] = low[:HALF].astype(BF)
        s2s[n, 1, 0:HALF, :] = high[:HALF].astype(BF)
        s2s[n, 0, HALF:, :] = two(one(total[HALF:])).astype(BF)
        s2s[n, 1, HALF:, :] = two(one(total[HALF:])).astype(BF)
        for i in (1, 2, 3):
            pick = before(pb, (pb + i) % 4, backward).astype(jnp.int32)
            send(s2s.at[n, pick], s2r.at[n, i - 1], sc_send.at[n, 2], sc_recv.at[n, 3 + i], dev(0, i))
        return lower[:HALF], total[HALF:]

    def scan_last(n, backward, lower, extra):
        for i in (1, 2, 3):
            await_(s2r.at[n, i - 1], sc_recv.at[n, 3 + i])
        for i in (1, 2, 3):
            got = s2r[n, i - 1].astype(F32)
            flag = jnp.logical_or(c == 1, before((pb - i + 4) % 4, pb, backward))
            lower = lower + jnp.where(flag, got[:HALF], 0.0)
            extra = extra + got[HALF:]
        far = 0 if backward else 1
        fin[n] = (lower + jnp.where(o == far, kvs[n, own_half, :], 0.0)).astype(BF)
        send(fin.at[n], st.at[n, own_half], sc_send.at[n, 3], sc_recv.at[n, 7], sib)
        st[n, own_half, :] = (lower + jnp.where(c == far, s0r[n, 0:HALF, :], 0.0)).astype(BF)
        return one(extra)

    def scan_end(n):
        await_(fin.at[n], sc_recv.at[n, 7])

    def scan_drain(n):
        await_(s0s.at[n], sc_send.at[n, 0])
        await_(s1r.at[n], sc_send.at[n, 1])
        await_(s2r.at[n], sc_send.at[n, 2])
        await_(fin.at[n], sc_send.at[n, 3])

    def z_start(n):
        for i in range(1, 8):
            slot = zb.at[n, z]
            send(slot, slot, z_send.at[n], z_recv.at[n, i - 1], (s, (z + i) % 8))

    def z_end(n):
        for i in range(1, 8):
            await_(zb.at[n, z], z_recv.at[n, i - 1])
        total = zb[n, 0]
        for i in range(1, 8):
            total = total + zb[n, i]
        return total

    def z_drain(n):
        await_(zb.at[n, pl.ds(0, 7)], z_send.at[n])

    low_rows, high_rows = pl.ds(0, HALF), pl.ds(HALF, HALF)

    def piece(da, db):
        return wall.at[2 * chip(da, db) + c]

    def piece_o(da, db):
        return wall.at[2 * chip_o(da, db) + o]

    def ag_full(ref, event, d):
        send(ref, ref, ag_send.at[0], ag_recv.at[event], d)

    def ag_pair(ref, i, j):
        send(ref, ref, ag_send.at[0], ag_sib.at[4 * i + j], sib)

    def ag_own():
        ref = piece(0, 0)
        ag_full(ref, 0, dev(1, 0))
        ag_full(ref, 1, dev(3, 0))
        ag_full(ref, 4, dev(0, 1))
        ag_full(ref, 5, dev(0, 3))
        ag_pair(ref, 0, 0)

    def ag_a(i):
        da = STEPS[i]
        ref = piece(da, 0)
        if i == 3:
            await_(ref.at[low_rows], ag_recv.at[2])
            await_(ref.at[high_rows], ag_recv.at[3])
        else:
            await_(ref, ag_recv.at[i - 1])
            part_rows = low_rows if i == 1 else high_rows
            half = ref.at[part_rows]
            send(half, half, ag_send.at[0], ag_recv.at[1 + i], dev(1 if i == 1 else 3, 0))
        ag_full(ref, 4 + 4 * i, dev(0, 1))
        ag_full(ref, 5 + 4 * i, dev(0, 3))
        ag_pair(ref, i, 0)

    def ag_b(i):
        da = STEPS[i]
        for j in (1, 2):
            ref = piece(da, STEPS[j])
            await_(ref, ag_recv.at[4 + 4 * i + j - 1])
            half = ref.at[low_rows if j == 1 else high_rows]
            send(half, half, ag_send.at[0], ag_recv.at[5 + 4 * i + j], dev(0, 1 if j == 1 else 3))
            ag_pair(ref, i, j)

    def ag_b_far(i):
        ref = piece(STEPS[i], 2)
        await_(ref.at[low_rows], ag_recv.at[6 + 4 * i])
        await_(ref.at[high_rows], ag_recv.at[7 + 4 * i])
        ag_pair(ref, i, 3)

    def ag_pair_end(j):
        for i in range(4):
            await_(piece_o(STEPS[i], STEPS[j]), ag_sib.at[4 * i + j])

    def ag_drain():
        await_(wall.at[pl.ds(0, 31)], ag_send.at[0])

    def upstream(j):
        mine = [2 * chip(STEPS[i], STEPS[j]) + c for i in range(4)]
        mine += [2 * chip_o(STEPS[i], STEPS[j]) + o for i in range(4)]
        grad = jnp.concatenate([og[:, head(m)] for m in mine], axis=1)
        for n in (0, HALF):
            weight = jnp.concatenate([wall[m, n:n + HALF, :] for m in mine], axis=1)
            term = nt(grad, weight)
            up[:, n:n + HALF] = term if j == 0 else up[:, n:n + HALF] + term

    def ordered(j):
        return jnp.where(j == 0, 2, jnp.where(j == 3, 0, jnp.where(j == 1, 1, 3)))

    def rs_pair_out():
        def pair(i, _):
            jb, h = i // 2, i % 2
            db = ordered(jb)
            m0 = 2 * chip_o(ordered(2 * h), db) + o
            m1 = 2 * chip_o(ordered(2 * h + 1), db) + o
            term = nn(n_t[...], jnp.concatenate([og[:, head(m0)], og[:, head(m1)]], axis=1))
            sib_out[2 * i] = term[:, :HD].astype(BF)
            sib_out[2 * i + 1] = term[:, HD:].astype(BF)
            slot = pl.ds(2 * i, 2)
            send(sib_out.at[slot], sib_in.at[slot], pair_send.at[0], pair_recv.at[i], sib)
            return _

        lax.fori_loop(0, 8, pair, 0)

    def rs_send_to(src, dst, rsem, d):
        send(src, dst, rs_send.at[0], rsem, d)

    def rs_own():
        def group(jb, _):
            db = ordered(jb)
            for h in (0, 1):
                m0 = 2 * chip(ORDER[2 * h], db) + c
                m1 = 2 * chip(ORDER[2 * h + 1], db) + c
                term = nn(n_t[...], jnp.concatenate([og[:, head(m0)], og[:, head(m1)]], axis=1))
                i = 2 * jb + h
                await_(sib_in.at[pl.ds(2 * i, 2)], pair_recv.at[i])
                part[2 * i] = (term[:, :HD] + sib_in[2 * i].astype(F32)).astype(BF)
                part[2 * i + 1] = (term[:, HD:] + sib_in[2 * i + 1].astype(F32)).astype(BF)
                if h == 0:
                    far, near = part.at[2 * i], part.at[2 * i + 1]
                    rs_send_to(far.at[low_rows], ra.at[jb, 0], rs_recv.at[jb, 0], dev(1, 0))
                    rs_send_to(far.at[high_rows], ra.at[jb, 1], rs_recv.at[jb, 1], dev(3, 0))
                    rs_send_to(near.at[high_rows], ra.at[jb, 2], rs_recv.at[jb, 2], dev(1, 0))
                else:
                    near = part.at[2 * i]
                    rs_send_to(near.at[low_rows], ra.at[jb, 4], rs_recv.at[jb, 4], dev(3, 0))
            return _

        lax.fori_loop(0, 4, group, 0)

    def rs_a_mid(jb):
        await_(ra.at[jb, 0], rs_recv.at[jb, 0])
        m = 4 * jb + 1
        part[m, 0:HALF, :] = (part[m, 0:HALF, :].astype(F32) + ra[jb, 0].astype(F32)).astype(BF)
        rs_send_to(part.at[m, low_rows], ra.at[jb, 3], rs_recv.at[jb, 3], dev(1, 0))
        await_(ra.at[jb, 1], rs_recv.at[jb, 1])
        m = 4 * jb + 2
        part[m, HALF:, :] = (part[m, HALF:, :].astype(F32) + ra[jb, 1].astype(F32)).astype(BF)
        rs_send_to(part.at[m, high_rows], ra.at[jb, 5], rs_recv.at[jb, 5], dev(3, 0))

    def rs_a_end(jb):
        for i in (2, 3, 4, 5):
            await_(ra.at[jb, i], rs_recv.at[jb, i])
        m = 4 * jb + 3
        top = part[m, 0:HALF, :].astype(F32) + ra[jb, 3].astype(F32) + ra[jb, 4].astype(F32)
        low = part[m, HALF:, :].astype(F32) + ra[jb, 2].astype(F32) + ra[jb, 5].astype(F32)
        if jb == 3:
            wg_o[0:HALF, :] = top
            wg_o[HALF:, :] = low
            return
        pb_buf[jb, 0:HALF, :] = top.astype(BF)
        pb_buf[jb, HALF:, :] = low.astype(BF)
        ref = pb_buf.at[jb]
        if jb == 0:
            rs_send_to(ref.at[low_rows], rb.at[0], rsb_recv.at[0], dev(0, 1))
            rs_send_to(ref.at[high_rows], rb.at[1], rsb_recv.at[1], dev(0, 3))
        elif jb == 1:
            rs_send_to(ref.at[high_rows], rb.at[2], rsb_recv.at[2], dev(0, 1))
        else:
            rs_send_to(ref.at[low_rows], rb.at[4], rsb_recv.at[4], dev(0, 3))

    def rs_b_mid():
        await_(rb.at[0], rsb_recv.at[0])
        pb_buf[1, 0:HALF, :] = (pb_buf[1, 0:HALF, :].astype(F32) + rb[0].astype(F32)).astype(BF)
        rs_send_to(pb_buf.at[1, low_rows], rb.at[3], rsb_recv.at[3], dev(0, 1))
        await_(rb.at[1], rsb_recv.at[1])
        pb_buf[2, HALF:, :] = (pb_buf[2, HALF:, :].astype(F32) + rb[1].astype(F32)).astype(BF)
        rs_send_to(pb_buf.at[2, high_rows], rb.at[5], rsb_recv.at[5], dev(0, 3))

    def rs_b_end():
        for i in (2, 3, 4, 5):
            await_(rb.at[i], rsb_recv.at[i])
        wg_o[0:HALF, :] = wg_o[0:HALF, :] + rb[3].astype(F32) + rb[4].astype(F32)
        wg_o[HALF:, :] = wg_o[HALF:, :] + rb[2].astype(F32) + rb[5].astype(F32)

    def rs_drain():
        await_(sib_in.at[pl.ds(0, 15)], rs_send.at[0])
        await_(sib_out, pair_send.at[0])

    tri_r = lax.broadcasted_iota(jnp.int32, (HALF, HALF), 0)
    tri_u = lax.broadcasted_iota(jnp.int32, (HALF, HALF), 1)

    def lower_part(a, b):
        return jnp.where(tri_u <= tri_r, nt(a, b), 0.0).astype(BF)

    def upper_part(a, b):
        return jnp.where(tri_u >= tri_r, nt(a, b), 0.0).astype(BF)

    top, bot = slice(0, HALF), slice(HALF, TOK)

    def forward_head(h):
        l = head(h)
        q0, q1, k0, k1 = q[top, l], q[bot, l], k[top, l], k[bot, l]
        att[top, l] = nn(lower_part(q0, k0), v[top, l])
        both = jnp.concatenate([nt(q1, k0).astype(BF), lower_part(q1, k1)], axis=1)
        att[bot, l] = nn(both, v[:, l])
        scores_t[h, top, top] = upper_part(k0, q0)
        scores_t[h, top, bot] = nt(k0, q1).astype(BF)
        scores_t[h, bot, bot] = upper_part(k1, q1)

    def back_head(h):
        l = head(h)
        p0, p1, v0, v1 = p[top, l], p[bot, l], v[top, l], v[bot, l]
        state = st[0, rows(h), :]
        dq_o[top, l] = (nn(lower_part(p0, v0), k[top, l]) + nt(p0, state)).astype(BF)
        both = jnp.concatenate([nt(p1, v0).astype(BF), lower_part(p1, v1)], axis=1)
        dq_o[bot, l] = (nn(both, k[:, l]) + nt(p1, state)).astype(BF)
        both = jnp.concatenate([upper_part(v0, p0), nt(v0, p1).astype(BF)], axis=1)
        dkp[top, l] = nn(both, q[:, l])
        dkp[bot, l] = nn(upper_part(v1, p1), q[bot, l])
        dvp[top, l] = nn(scores_t[h, top, :], p[:, l])
        dvp[bot, l] = nn(scores_t[h, bot, bot], p1)

    def loop(lo, hi, f):
        def step(h, _):
            f(h)
            return _

        lax.fori_loop(lo, hi, step, 0)

    lane4 = lax.broadcasted_iota(jnp.int32, (NH, HD), 1)
    placed = jnp.zeros((NH, HD), F32)
    for j in range(4):
        placed = placed + jnp.where(lane4 == 4 * s + j, gain_ref[:, j:j + 1].astype(F32), 0.0)
    placed = jnp.concatenate([placed, jnp.zeros((16 - NH, HD), F32)], axis=0)
    loads[2].wait()
    pl.semaphore_wait(barrier, 14)
    ag_own()
    loads[0].wait()
    loads[1].wait()
    for h in range(NH):
        l = slice(h * HD, (h + 1) * HD)
        kvs[0, l, :] = tn(k[:, l], v[:, l])
    scan_start(0, placed)
    loads[3].wait()
    loop(0, 1, forward_head)
    scan_ring_a(0, placed)
    loop(1, 2, forward_head)
    ag_a(1)
    ag_a(2)
    loop(2, 3, forward_head)
    lower, extra = scan_ring_b(0, False)
    loop(3, 4, forward_head)
    ag_a(3)
    ag_b(0)
    gains = scan_last(0, False, lower, extra)
    for h in range(NH):
        gflat[0:1, h * HD:(h + 1) * HD] = gains[h:h + 1]
        q_t[h] = q[:, h * HD:(h + 1) * HD].T
    ag_b_far(0)
    scan_end(0)

    for h in range(NH):
        l = slice(h * HD, (h + 1) * HD)
        a = att[:, l] + nn(q[:, l], st[0, l, :])
        att[:, l] = a
        col[0] = a * a if h == 0 else col[0] + a * a
    for t in range(4):
        l = slice(t * 128, (t + 1) * 128)
        zb[0, z, t:t + 1, :] = to_rows(jnp.sum(col[0, l, :], axis=1, keepdims=True))
    z_start(0)
    ag_b(1)
    ag_b(2)
    loads[4].wait()
    ag_pair_end(0)
    upstream(0)
    ag_b_far(1)
    ag_b(3)
    ag_b_far(2)
    ag_pair_end(1)
    upstream(1)
    ag_b_far(3)
    ag_pair_end(2)
    upstream(2)
    ag_pair_end(3)
    upstream(3)

    def inner_block(t, _):
        r = rows(t, 128)
        total = jnp.zeros((HD, HD), F32)
        for h in range(NH):
            l = slice(h * HD, (h + 1) * HD)
            total = total + up[r, l] * gflat[0:1, l] * att[r, l]
        zb[1, z, pl.ds(t, 1), :] = to_rows(jnp.sum(total, axis=1, keepdims=True))
        return _

    lax.fori_loop(0, 4, inner_block, 0)
    z_start(1)
    squares = z_end(0)
    inv = lax.rsqrt(squares / D + EPSILON)
    for t in range(4):
        col[0, t * 128:(t + 1) * 128, :] = jnp.broadcast_to(to_column(inv[t:t + 1]), (HD, HD))

    def normed_block(t, _):
        r = rows(t, 128)
        for h in range(NH):
            l = slice(h * HD, (h + 1) * HD)
            normed = att[r, l] * col[0, r, :] * gflat[0:1, l]
            n_t[l, head(t)] = normed.astype(BF).T
        return _

    lax.fori_loop(0, 4, normed_block, 0)
    rs_pair_out()
    rs_own()
    inner = z_end(1)
    for t in range(4):
        pair = inv[t:t + 1] * inv[t:t + 1] * inv[t:t + 1] * inner[t:t + 1] / D
        col[1, t * 128:(t + 1) * 128, :] = jnp.broadcast_to(to_column(pair), (HD, HD))

    def grad_block(t, sums):
        r = rows(t, 128)
        out = []
        for h in range(NH):
            l = slice(h * HD, (h + 1) * HD)
            a, u, i = att[r, l], up[r, l], col[0, r, :]
            p[r, l] = (i * u * gflat[0:1, l] - a * col[1, r, :]).astype(BF)
            out.append(sums[h] + jnp.sum(u * a * i, axis=0, keepdims=True))
        return tuple(out)

    sums = lax.fori_loop(0, 4, grad_block, (jnp.zeros((1, HD), F32),) * NH)
    gain_part = jnp.concatenate(list(sums), axis=0)

    for h in range(NH):
        l = slice(h * HD, (h + 1) * HD)
        kvs[1, l, :] = nn(q_t[h], p[:, l])
    scan_start(1, two(gain_part))
    rs_a_mid(0)
    loop(0, 1, back_head)
    scan_ring_a(1, two(gain_part))
    rs_a_mid(1)
    rs_a_mid(2)
    loop(1, 2, back_head)
    lower, extra = scan_ring_b(1, True)
    rs_a_mid(3)
    rs_a_end(0)
    loop(2, 3, back_head)
    rs_a_end(1)
    gain_total = scan_last(1, True, lower, extra)
    loop(3, 4, back_head)
    dq_copy = pltpu.make_async_copy(dq_o, dq_hbm, out_sem.at[0])
    dq_copy.start()
    rs_a_end(2)
    rs_b_mid()
    for j in range(4):
        gg_ref[:, j:j + 1] = jnp.sum(
            jnp.where(lane4 == 4 * s + j, gain_total, 0.0), axis=1, keepdims=True
        )
    scan_end(1)
    for h in range(NH):
        l = slice(h * HD, (h + 1) * HD)
        dk_o[:, l] = (dkp[:, l] + nt(v[:, l], st[1, l, :])).astype(BF)
        dv_o[:, l] = (dvp[:, l] + nn(k[:, l], st[1, l, :])).astype(BF)
    dk_copy = pltpu.make_async_copy(dk_o, dk_hbm, out_sem.at[1])
    dv_copy = pltpu.make_async_copy(dv_o, dv_hbm, out_sem.at[2])
    dk_copy.start()
    dv_copy.start()
    ag_drain()
    scan_drain(0)
    z_drain(0)
    z_drain(1)
    rs_a_end(3)
    rs_b_end()
    wg_copy = pltpu.make_async_copy(wg_o, wg_hbm, out_sem.at[3])
    wg_copy.start()
    rs_drain()
    scan_drain(1)
    for copy in (dq_copy, dk_copy, dv_copy, wg_copy):
        copy.wait()


def copy_kernel(a, b, d, e, f, a_o, b_o, d_o, e_o, f_o, sem):
    copies = [
        pltpu.make_async_copy(src, dst, sem.at[i])
        for i, (src, dst) in enumerate([(a, a_o), (b, b_o), (d, d_o), (e, e_o), (f, f_o)])
    ]
    for copy in copies:
        copy.start()
    for copy in copies:
        copy.wait()


def body(queries, keys, values, out_grad, gain, out_weight):
    any_space = pl.BlockSpec(memory_space=pl.ANY)
    hbm = pl.BlockSpec(memory_space=pltpu.HBM)
    vmem = pl.BlockSpec(memory_space=pltpu.VMEM)
    sem = pltpu.SemaphoreType.DMA
    outs = (
        jax.ShapeDtypeStruct((TOK, WID), BF),
        jax.ShapeDtypeStruct((TOK, WID), BF),
        jax.ShapeDtypeStruct((TOK, WID), BF),
        jax.ShapeDtypeStruct((WID, HD), F32),
        jax.ShapeDtypeStruct((NH, 4), F32),
    )
    wide = lambda dt: pltpu.VMEM((TOK, WID), dt)
    results = pl.pallas_call(
        layer_kernel,
        out_shape=outs,
        in_specs=[hbm, hbm, hbm, hbm, vmem, hbm],
        out_specs=(any_space, any_space, any_space, any_space, vmem),
        scratch_shapes=[
            wide(BF), wide(BF), wide(BF),
            pltpu.VMEM((TOK, D), BF),
            pltpu.VMEM((32, WID, HD), BF),
            pltpu.VMEM((NH, TOK, TOK), BF),
            pltpu.VMEM((NH, HD, TOK), BF),
            wide(F32), wide(F32), wide(BF), wide(BF), wide(F32), wide(F32),
            wide(BF), wide(BF), wide(BF),
            pltpu.VMEM((WID, HD), F32),
            pltpu.VMEM((2, WID, HD), F32),
            pltpu.VMEM((2, HALF + 16, HD), F32),
            pltpu.VMEM((2, HALF + 16, HD), F32),
            pltpu.VMEM((2, HALF + 16, HD), BF),
            pltpu.VMEM((2, 3, HALF + 16, HD), BF),
            pltpu.VMEM((2, 2, HALF + 16, HD), BF),
            pltpu.VMEM((2, 3, HALF + 16, HD), BF),
            pltpu.VMEM((2, HALF, HD), BF),
            pltpu.VMEM((2, WID, HD), BF),
            pltpu.VMEM((2, 8, 4, HD), F32),
            pltpu.VMEM((1, WID), F32),
            pltpu.VMEM((2, TOK, HD), F32),
            pltpu.VMEM((16, WID, HD), BF),
            pltpu.VMEM((16, WID, HD), BF),
            pltpu.VMEM((16, WID, HD), BF),
            pltpu.VMEM((4, 6, HALF, HD), BF),
            pltpu.VMEM((3, WID, HD), BF),
            pltpu.VMEM((6, HALF, HD), BF),
            sem((5,)), sem((4,)), sem((1,)), sem((20,)), sem((16,)),
            sem((2, 4)), sem((2, 8)), sem((2,)), sem((2, 7)),
            sem((1,)), sem((4, 6)), sem((6,)), sem((1,)), sem((8,)),
        ],
        compiler_params=pltpu.CompilerParams(
            collective_id=0, has_side_effects=True, vmem_limit_bytes=52 * 2**20
        ),
        cost_estimate=pl.CostEstimate(
            flops=6_400_000_000, bytes_accessed=8_000_000, transcendentals=512
        ),
        name="layer",
    )(queries, keys, values, out_grad, gain, out_weight)
    return pl.pallas_call(
        copy_kernel,
        out_shape=outs,
        in_specs=[any_space] * 5,
        out_specs=(hbm,) * 5,
        scratch_shapes=[sem((5,))],
        compiler_params=pltpu.CompilerParams(vmem_limit_bytes=2**20),
        name="results",
    )(*results)


def solution(mesh):
    return jax.shard_map(
        body,
        mesh=mesh,
        in_specs=(
            P("seq", "dp"),
            P("seq", "dp"),
            P("seq", "dp"),
            P("seq", None),
            P("dp", "seq"),
            P("dp", "seq"),
        ),
        out_specs=(P("seq", "dp"), P("seq", "dp"), P("seq", "dp"), P("dp", "seq"), P("dp", "seq")),
        check_vma=False,
    )
```

time: 324 us -> 64 us (0.20)
  blocking collectives: 120 us -> 0 us
  other arithmetic: 67.7 us -> 0 us
  waiting for transfers between devices: 66.2 us -> 0 us
  Pallas kernels: 0 us -> 61.3 us
  matrix products: 32.3 us -> 0 us
  local copies, waits for them, and re-layouts: 18.6 us -> 1.58 us
  between operations: 14.6 us -> 0.65 us
    unnamed x1 -> x0, blocking collectives: 66.7 us -> none
    select_n x62 -> x0, other arithmetic: 64.8 us -> none  [step(): return jnp.where(position < mine, longer, so_far)]
    pallas_call x0 -> x2, Pallas kernels: none -> 61.3 us  [the longest x1 60 us: body(): pl.pallas_call(layer_kernel, out_shape=outs, in_specs=[hbm, hbm, hbm, hbm...]
    all_gather x3 -> x0, waiting for transfers between devices: 36.7 us -> none  [the longest x2 30.1 us: prefix(): pieces = lax.all_gather(value, axis)]
    dot_general x14 -> x0, matrix products: 32.3 us -> none  [the longest x1 7.93 us: body(): jnp.einsum('tf,tc->fc', normed, out_grad, preferred_element_type=jnp.floa...]
    reduce_scatter x1 -> x0, waiting for transfers between devices: 28.8 us -> none  [body(): lax.psum_scatter(weight_term, 'seq', scatter_dimension=1, tiled=True)]
    psum x2 -> x0, blocking collectives: 27.9 us -> none  [the longest x1 14.1 us: body(): squares = lax.psum(squares_local, 'dp')]
    all_gather x1 -> x0, blocking collectives: 25.8 us -> none  [body(): lax.all_gather(gain, 'seq', axis=1, tiled=True)]
  transfers between devices with their start and end apart: 4 -> 0, of which waited for: 3 -> 0; matrix products, arithmetic and copies ran while one was open for 32% -> 0% of each run, Pallas kernels for 0% -> 0%
where the time goes in v1:
time: 64 us; the launch traced here: 63.5 us
  Pallas kernels  61.3 us (96%)
  local copies, waits for them, and re-layouts  1.58 us (2%)
  between operations  0.65 us (1%)
    pallas_call x1, Pallas kernels, body(): pl.pallas_call(layer_kernel, out_shape=outs, in_specs=[hbm, hbm, hbm, hbm...  60 us
    unnamed x4, local copies, waits for them, and re-layouts  1.58 us

profile of v1, /device:TPU:1, one launch (start us, length us, event | category | flops | bytes accessed | tf_op | source)
XLA Modules:
  0.0 63.5 jit_solution(17832378033379310520)
XLA Ops:
  0.6 0.0 copy-start
  0.6 0.9 %copy-done = bf16[512,128]{1,0:T(8,128)(2,1)S(1)} copy-done((bf16[512,128]{1,0:T(8,128)(2,1)S(1)}, bf16[512,128]{1,0:T(8,128)(2,1)}, u32[]{:S(2)}) %copy-start) | copy-done | bytes 131096
  1.5 0.0 copy-start.1
  1.5 0.7 %copy-done.1 = bf16[4,4]{1,0:T(4,128)(2,1)S(1)} copy-done((bf16[4,4]{1,0:T(4,128)(2,1)S(1)}, bf16[4,4]{1,0:T(4,128)(2,1)}, u32[]{:S(2)}) %copy-start.1) | copy-done | bytes 56
  2.2 60.0 %layer.1 = (bf16[512,512]{1,0:T(8,128)(2,1)S(1)}, bf16[512,512]{1,0:T(8,128)(2,1)S(1)}, bf16[512,512]{1,0:T(8,128)(2,1)S(1)}, f32[512,128]{1,0:T(8,128)S(1)}, f32[4,4]{1,0:T(4,128)S(1)}) custom-call(bf16[512,512]{1,0:T(8,128)(2,1)} %q_hbm.1, bf16[512,512]{1,0:T(8,128)(2,1)} %k_hbm.1, bf16[512,512]{1,0:T(8,128)(2,1)} %v_hbm.1, bf16[512,4096]{1,0:T(8,128)(2,1)} %og_hbm.1, ...), custom_call_target="tpu_custom_call" | custom-call | flops 6400000000 | bytes 8000000 | tf_op jit(solution)/shard_map/layer/pallas_call | solution.py:563
  62.2 1.3 %results.1 = (bf16[512,512]{1,0:T(8,128)(2,1)}, bf16[512,512]{1,0:T(8,128)(2,1)}, bf16[512,512]{1,0:T(8,128)(2,1)}, f32[512,128]{1,0:T(8,128)}, f32[4,4]{1,0:T(4,128)}) custom-call(bf16[512,512]{1,0:T(8,128)(2,1)S(1)} %get-tuple-element.10.a, bf16[512,512]{1,0:T(8,128)(2,1)S(1)} %get-tuple-element.11.b, bf16[512,512]{1,0:T(8,128)(2,1)S(1)} %get-tuple-element.12.d, ...), custom_call_target="tpu_custom_call" | custom-call | tf_op jit(solution)/shard_map/results/pallas_call | solution.py:607
Async XLA Ops:
  0.6 0.9 %copy-start = (bf16[512,128]{1,0:T(8,128)(2,1)S(1)}, bf16[512,128]{1,0:T(8,128)(2,1)}, u32[]{:S(2)}) copy-start(bf16[512,128]{1,0:T(8,128)(2,1)} %w_hbm.1) | copy-start | bytes 393220
  1.5 0.7 %copy-start.1 = (bf16[4,4]{1,0:T(4,128)(2,1)S(1)}, bf16[4,4]{1,0:T(4,128)(2,1)}, u32[]{:S(2)}) copy-start(bf16[4,4]{1,0:T(4,128)(2,1)} %gain_ref.1) | copy-start | bytes 100

commit v2 on v1

--- a/solution.py
+++ b/solution.py
@@ -192,49 +192,117 @@
     def piece_o(da, db):
         return wall.at[2 * chip_o(da, db) + o]
 
-    def ag_full(ref, event, d):
-        send(ref, ref, ag_send.at[0], ag_recv.at[event], d)
+    halves = (low_rows, high_rows)
+
+    def ag_half(ref, half, event, d):
+        part_ref = ref.at[halves[half]]
+        send(part_ref, part_ref, ag_send.at[0], ag_recv.at[event], d)
+
+    def ag_wait(ref, half, event):
+        await_(ref.at[halves[half]], ag_recv.at[event])
 
     def ag_pair(ref, i, j):
         send(ref, ref, ag_send.at[0], ag_sib.at[4 * i + j], sib)
 
     def ag_own():
         ref = piece(0, 0)
-        ag_full(ref, 0, dev(1, 0))
-        ag_full(ref, 1, dev(3, 0))
-        ag_full(ref, 4, dev(0, 1))
-        ag_full(ref, 5, dev(0, 3))
+        ag_half(ref, 0, 0, dev(1, 0))
+        ag_half(ref, 1, 3, dev(3, 0))
+        ag_half(ref, 1, 1, dev(1, 0))
+        ag_half(ref, 0, 2, dev(3, 0))
+
+    def ag_own_b():
+        ref = piece(0, 0)
+        ag_half(ref, 0, 6, dev(0, 1))
+        ag_half(ref, 1, 9, dev(0, 3))
+        ag_half(ref, 1, 7, dev(0, 1))
+        ag_half(ref, 0, 8, dev(0, 3))
         ag_pair(ref, 0, 0)
 
-    def ag_a(i):
-        da = STEPS[i]
-        ref = piece(da, 0)
-        if i == 3:
-            await_(ref.at[low_rows], ag_recv.at[2])
-            await_(ref.at[high_rows], ag_recv.at[3])
-        else:
-            await_(ref, ag_recv.at[i - 1])
-            part_rows = low_rows if i == 1 else high_rows
-            half = ref.at[part_rows]
-            send(half, half, ag_send.at[0], ag_recv.at[1 + i], dev(1 if i == 1 else 3, 0))
-        ag_full(ref, 4 + 4 * i, dev(0, 1))
-        ag_full(ref, 5 + 4 * i, dev(0, 3))
-        ag_pair(ref, i, 0)
-
-    def ag_b(i):
-        da = STEPS[i]
-        for j in (1, 2):
-            ref = piece(da, STEPS[j])
-            await_(ref, ag_recv.at[4 + 4 * i + j - 1])
-            half = ref.at[low_rows if j == 1 else high_rows]
-            send(half, half, ag_send.at[0], ag_recv.at[5 + 4 * i + j], dev(0, 1 if j == 1 else 3))
-            ag_pair(ref, i, j)
+    def ag_both(ref, i, half):
+        ag_half(ref, half, 6 + 6 * i + half, dev(0, 1))
+        ag_half(ref, half, 8 + 6 * i + half, dev(0, 3))
+
+    def ag_a_first():
+        ref = piece(3, 0)
+        ag_wait(ref, 0, 0)
+        ag_half(ref, 0, 4, dev(1, 0))
+        ag_both(ref, 1, 0)
+        ref = piece(1, 0)
+        ag_wait(ref, 1, 3)
+        ag_half(ref, 1, 5, dev(3, 0))
+        ag_both(ref, 2, 1)
+
+    def ag_a_rest():
+        ref = piece(3, 0)
+        ag_wait(ref, 1, 1)
+        ag_both(ref, 1, 1)
+        ag_pair(ref, 1, 0)
+        ref = piece(1, 0)
+        ag_wait(ref, 0, 2)
+        ag_both(ref, 2, 0)
+        ag_pair(ref, 2, 0)
+
+    def ag_a_far():
+        ref = piece(2, 0)
+        ag_wait(ref, 0, 4)
+        ag_both(ref, 3, 0)
+        ag_wait(ref, 1, 5)
+        ag_both(ref, 3, 1)
+        ag_pair(ref, 3, 0)
+
+    def ag_b_up(i):
+        ref = piece(STEPS[i], 3)
+        ag_wait(ref, 0, 6 + 6 * i)
+        ag_half(ref, 0, 10 + 6 * i, dev(0, 1))
+
+    def ag_b_down(i):
+        ref = piece(STEPS[i], 1)
+        ag_wait(ref, 1, 9 + 6 * i)
+        ag_half(ref, 1, 11 + 6 * i, dev(0, 3))
+
+    def ag_b_rest(i):
+        ref = piece(STEPS[i], 3)
+        ag_wait(ref, 1, 7 + 6 * i)
+        ag_pair(ref, i, 1)
+        ref = piece(STEPS[i], 1)
+        ag_wait(ref, 0, 8 + 6 * i)
+        ag_pair(ref, i, 2)
 
     def ag_b_far(i):
         ref = piece(STEPS[i], 2)
-        await_(ref.at[low_rows], ag_recv.at[6 + 4 * i])
-        await_(ref.at[high_rows], ag_recv.at[7 + 4 * i])
+        ag_wait(ref, 0, 10 + 6 * i)
+        ag_wait(ref, 1, 11 + 6 * i)
         ag_pair(ref, i, 3)
+
+    def ag_1():
+        ag_a_first()
+        ag_b_up(0)
+        ag_b_down(0)
+
+    def ag_2():
+        ag_a_rest()
+        ag_a_far()
+
+    def ag_3():
+        ag_b_rest(0)
+        ag_b_up(1)
+        ag_b_down(2)
+        ag_b_down(1)
+        ag_b_up(2)
+
+    def ag_4():
+        ag_b_far(0)
+        ag_b_up(3)
+        ag_b_down(3)
+        ag_b_rest(1)
+        ag_b_rest(2)
+
+    def ag_5():
+        ag_b_far(1)
+        ag_b_far(2)
+        ag_b_rest(3)
+        ag_b_far(3)
 
     def ag_pair_end(j):
         for i in range(4):
@@ -255,7 +323,7 @@
     def ordered(j):
         return jnp.where(j == 0, 2, jnp.where(j == 3, 0, jnp.where(j == 1, 1, 3)))
 
-    def rs_pair_out():
+    def rs_pair_out(lo, hi):
         def pair(i, _):
             jb, h = i // 2, i % 2
             db = ordered(jb)
@@ -268,12 +336,12 @@
             send(sib_out.at[slot], sib_in.at[slot], pair_send.at[0], pair_recv.at[i], sib)
             return _
 
-        lax.fori_loop(0, 8, pair, 0)
+        lax.fori_loop(lo, hi, pair, 0)
 
     def rs_send_to(src, dst, rsem, d):
         send(src, dst, rs_send.at[0], rsem, d)
 
-    def rs_own():
+    def rs_own(lo, hi):
         def group(jb, _):
             db = ordered(jb)
             for h in (0, 1):
@@ -294,7 +362,7 @@
                     rs_send_to(near.at[low_rows], ra.at[jb, 4], rs_recv.at[jb, 4], dev(3, 0))
             return _
 
-        lax.fori_loop(0, 4, group, 0)
+        lax.fori_loop(lo, hi, group, 0)
 
     def rs_a_mid(jb):
         await_(ra.at[jb, 0], rs_recv.at[jb, 0])
@@ -401,21 +469,20 @@
         kvs[0, l, :] = tn(k[:, l], v[:, l])
     scan_start(0, placed)
     loads[3].wait()
+    scan_ring_a(0, placed)
+    ag_own_b()
     loop(0, 1, forward_head)
-    scan_ring_a(0, placed)
-    loop(1, 2, forward_head)
-    ag_a(1)
-    ag_a(2)
-    loop(2, 3, forward_head)
+    ag_1()
+    loop(1, 3, forward_head)
     lower, extra = scan_ring_b(0, False)
+    ag_2()
     loop(3, 4, forward_head)
-    ag_a(3)
-    ag_b(0)
     gains = scan_last(0, False, lower, extra)
+    ag_3()
     for h in range(NH):
         gflat[0:1, h * HD:(h + 1) * HD] = gains[h:h + 1]
         q_t[h] = q[:, h * HD:(h + 1) * HD].T
-    ag_b_far(0)
+    ag_4()
     scan_end(0)
 
     for h in range(NH):
@@ -427,17 +494,12 @@
         l = slice(t * 128, (t + 1) * 128)
         zb[0, z, t:t + 1, :] = to_rows(jnp.sum(col[0, l, :], axis=1, keepdims=True))
     z_start(0)
-    ag_b(1)
-    ag_b(2)
     loads[4].wait()
     ag_pair_end(0)
     upstream(0)
-    ag_b_far(1)
-    ag_b(3)
-    ag_b_far(2)
+    ag_5()
     ag_pair_end(1)
     upstream(1)
-    ag_b_far(3)
     ag_pair_end(2)
     upstream(2)
     ag_pair_end(3)
@@ -468,8 +530,12 @@
         return _
 
     lax.fori_loop(0, 4, normed_block, 0)
-    rs_pair_out()
-    rs_own()
+    rs_pair_out(0, 4)
+    rs_own(0, 1)
+    rs_pair_out(4, 6)
+    rs_own(1, 2)
+    rs_pair_out(6, 8)
+    rs_own(2, 4)
     inner = z_end(1)
     for t in range(4):
         pair = inv[t:t + 1] * inv[t:t + 1] * inv[t:t + 1] * inner[t:t + 1] / D
@@ -492,23 +558,23 @@
         l = slice(h * HD, (h + 1) * HD)
         kvs[1, l, :] = nn(q_t[h], p[:, l])
     scan_start(1, two(gain_part))
-    rs_a_mid(0)
     loop(0, 1, back_head)
     scan_ring_a(1, two(gain_part))
+    rs_a_mid(0)
     rs_a_mid(1)
     rs_a_mid(2)
+    rs_a_mid(3)
     loop(1, 2, back_head)
     lower, extra = scan_ring_b(1, True)
-    rs_a_mid(3)
     rs_a_end(0)
+    rs_a_end(1)
     loop(2, 3, back_head)
-    rs_a_end(1)
     gain_total = scan_last(1, True, lower, extra)
+    rs_a_end(2)
+    rs_b_mid()
     loop(3, 4, back_head)
     dq_copy = pltpu.make_async_copy(dq_o, dq_hbm, out_sem.at[0])
     dq_copy.start()
-    rs_a_end(2)
-    rs_b_mid()
     for j in range(4):
         gg_ref[:, j:j + 1] = jnp.sum(
             jnp.where(lane4 == 4 * s + j, gain_total, 0.0), axis=1, keepdims=True
@@ -592,7 +658,7 @@
             pltpu.VMEM((4, 6, HALF, HD), BF),
             pltpu.VMEM((3, WID, HD), BF),
             pltpu.VMEM((6, HALF, HD), BF),
-            sem((5,)), sem((4,)), sem((1,)), sem((20,)), sem((16,)),
+            sem((5,)), sem((4,)), sem((1,)), sem((30,)), sem((16,)),
             sem((2, 4)), sem((2, 8)), sem((2,)), sem((2, 7)),
             sem((1,)), sem((4, 6)), sem((6,)), sem((1,)), sem((8,)),
         ],

time: 64 us -> 58.4 us (0.912)
  Pallas kernels: 61.3 us -> 55.9 us
    pallas_call x1, Pallas kernels: 60 us -> 54.6 us  [body(): pl.pallas_call(layer_kernel, out_shape=outs, in_specs=[hbm, hbm, hbm, hbm...]
where the time goes in v2:
time: 58.4 us; the launch traced here: 58.1 us
  Pallas kernels  55.9 us (96%)
  local copies, waits for them, and re-layouts  1.58 us (3%)
  between operations  0.65 us (1%)
    pallas_call x1, Pallas kernels, body(): pl.pallas_call(layer_kernel, out_shape=outs, in_specs=[hbm, hbm, hbm, hbm...  54.6 us
    unnamed x4, local copies, waits for them, and re-layouts  1.58 us
    pallas_call x1, Pallas kernels, body(): pl.pallas_call(copy_kernel, out_shape=outs, in_specs=[any_space] * 5, out...  1.27 us

profile of v2, /device:TPU:1, one launch (start us, length us, event | category | flops | bytes accessed | tf_op | source)
XLA Modules:
  0.0 58.1 jit_solution(1691959361555784944)
XLA Ops:
  0.6 0.0 copy-start
  0.6 0.9 %copy-done = bf16[512,128]{1,0:T(8,128)(2,1)S(1)} copy-done((bf16[512,128]{1,0:T(8,128)(2,1)S(1)}, bf16[512,128]{1,0:T(8,128)(2,1)}, u32[]{:S(2)}) %copy-start) | copy-done | bytes 131096
  1.5 0.0 copy-start.1
  1.5 0.7 %copy-done.1 = bf16[4,4]{1,0:T(4,128)(2,1)S(1)} copy-done((bf16[4,4]{1,0:T(4,128)(2,1)S(1)}, bf16[4,4]{1,0:T(4,128)(2,1)}, u32[]{:S(2)}) %copy-start.1) | copy-done | bytes 56
  2.2 54.6 %layer.1 = (bf16[512,512]{1,0:T(8,128)(2,1)S(1)}, bf16[512,512]{1,0:T(8,128)(2,1)S(1)}, bf16[512,512]{1,0:T(8,128)(2,1)S(1)}, f32[512,128]{1,0:T(8,128)S(1)}, f32[4,4]{1,0:T(4,128)S(1)}) custom-call(bf16[512,512]{1,0:T(8,128)(2,1)} %q_hbm.1, bf16[512,512]{1,0:T(8,128)(2,1)} %k_hbm.1, bf16[512,512]{1,0:T(8,128)(2,1)} %v_hbm.1, bf16[512,4096]{1,0:T(8,128)(2,1)} %og_hbm.1, ...), custom_call_target="tpu_custom_call" | custom-call | flops 6400000000 | bytes 8000000 | tf_op jit(solution)/shard_map/layer/pallas_call | solution.py:629
  56.8 1.3 %results.1 = (bf16[512,512]{1,0:T(8,128)(2,1)}, bf16[512,512]{1,0:T(8,128)(2,1)}, bf16[512,512]{1,0:T(8,128)(2,1)}, f32[512,128]{1,0:T(8,128)}, f32[4,4]{1,0:T(4,128)}) custom-call(bf16[512,512]{1,0:T(8,128)(2,1)S(1)} %get-tuple-element.10.a, bf16[512,512]{1,0:T(8,128)(2,1)S(1)} %get-tuple-element.11.b, bf16[512,512]{1,0:T(8,128)(2,1)S(1)} %get-tuple-element.12.d, ...), custom_call_target="tpu_custom_call" | custom-call | tf_op jit(solution)/shard_map/results/pallas_call | solution.py:673
Async XLA Ops:
  0.6 0.9 %copy-start = (bf16[512,128]{1,0:T(8,128)(2,1)S(1)}, bf16[512,128]{1,0:T(8,128)(2,1)}, u32[]{:S(2)}) copy-start(bf16[512,128]{1,0:T(8,128)(2,1)} %w_hbm.1) | copy-start | bytes 393220
  1.5 0.7 %copy-start.1 = (bf16[4,4]{1,0:T(4,128)(2,1)S(1)}, bf16[4,4]{1,0:T(4,128)(2,1)}, u32[]{:S(2)}) copy-start(bf16[4,4]{1,0:T(4,128)(2,1)} %gain_ref.1) | copy-start | bytes 100

commit v3 on v2

--- a/solution.py
+++ b/solution.py
@@ -120,7 +120,7 @@
         await_(s0r.at[n], sc_recv.at[n, 0])
         s1s[n, 0:HALF, :] = (kvs[n, own_half, :] + s0r[n, 0:HALF, :]).astype(BF)
         s1s[n, HALF:, :] = two(one(extra + s0r[n, HALF:, :])).astype(BF)
-        for i in (1, 2, 3):
+        for i in (2, 1, 3):
             send(s1s.at[n], s1r.at[n, i - 1], sc_send.at[n, 1], sc_recv.at[n, i], dev(i, 0))
 
     def scan_ring_b(n, backward):
@@ -140,7 +140,7 @@
         s2s[n, 1, 0:HALF, :] = high[:HALF].astype(BF)
         s2s[n, 0, HALF:, :] = two(one(total[HALF:])).astype(BF)
         s2s[n, 1, HALF:, :] = two(one(total[HALF:])).astype(BF)
-        for i in (1, 2, 3):
+        for i in (2, 1, 3):
             pick = before(pb, (pb + i) % 4, backward).astype(jnp.int32)
             send(s2s.at[n, pick], s2r.at[n, i - 1], sc_send.at[n, 2], sc_recv.at[n, 3 + i], dev(0, i))
         return lower[:HALF], total[HALF:]
@@ -169,7 +169,7 @@
         await_(fin.at[n], sc_send.at[n, 3])
 
     def z_start(n):
-        for i in range(1, 8):
+        for i in (4, 3, 5, 2, 6, 1, 7):
             slot = zb.at[n, z]
             send(slot, slot, z_send.at[n], z_recv.at[n, i - 1], (s, (z + i) % 8))
 
@@ -464,10 +464,11 @@
     ag_own()
     loads[0].wait()
     loads[1].wait()
-    for h in range(NH):
-        l = slice(h * HD, (h + 1) * HD)
-        kvs[0, l, :] = tn(k[:, l], v[:, l])
+    for i in (2 * o, 2 * o + 1):
+        kvs[0, rows(i), :] = tn(k[:, head(i)], v[:, head(i)])
     scan_start(0, placed)
+    for i in (2 * c, 2 * c + 1):
+        kvs[0, rows(i), :] = tn(k[:, head(i)], v[:, head(i)])
     loads[3].wait()
     scan_ring_a(0, placed)
     ag_own_b()
@@ -554,10 +555,11 @@
     sums = lax.fori_loop(0, 4, grad_block, (jnp.zeros((1, HD), F32),) * NH)
     gain_part = jnp.concatenate(list(sums), axis=0)
 
-    for h in range(NH):
-        l = slice(h * HD, (h + 1) * HD)
-        kvs[1, l, :] = nn(q_t[h], p[:, l])
+    for i in (2 * o, 2 * o + 1):
+        kvs[1, rows(i), :] = nn(q_t[i], p[:, head(i)])
     scan_start(1, two(gain_part))
+    for i in (2 * c, 2 * c + 1):
+        kvs[1, rows(i), :] = nn(q_t[i], p[:, head(i)])
     loop(0, 1, back_head)
     scan_ring_a(1, two(gain_part))
     rs_a_mid(0)

time: 58.4 us -> 57.7 us (0.988)
  Pallas kernels: 55.9 us -> 55.3 us
where the time goes in v3:
time: 57.7 us; the launch traced here: 57.5 us
  Pallas kernels  55.3 us (96%)
  local copies, waits for them, and re-layouts  1.58 us (3%)
  between operations  0.65 us (1%)
    pallas_call x1, Pallas kernels, body(): pl.pallas_call(layer_kernel, out_shape=outs, in_specs=[hbm, hbm, hbm, hbm...  54 us
    unnamed x4, local copies, waits for them, and re-layouts  1.58 us
    pallas_call x1, Pallas kernels, body(): pl.pallas_call(copy_kernel, out_shape=outs, in_specs=[any_space] * 5, out...  1.27 us

profile of v3, /device:TPU:1, one launch (start us, length us, event | category | flops | bytes accessed | tf_op | source)
XLA Modules:
  0.0 57.5 jit_solution(16972712996451776657)
XLA Ops:
  0.6 0.0 copy-start
  0.6 0.9 %copy-done = bf16[512,128]{1,0:T(8,128)(2,1)S(1)} copy-done((bf16[512,128]{1,0:T(8,128)(2,1)S(1)}, bf16[512,128]{1,0:T(8,128)(2,1)}, u32[]{:S(2)}) %copy-start) | copy-done | bytes 131096
  1.5 0.0 copy-start.1
  1.5 0.7 %copy-done.1 = bf16[4,4]{1,0:T(4,128)(2,1)S(1)} copy-done((bf16[4,4]{1,0:T(4,128)(2,1)S(1)}, bf16[4,4]{1,0:T(4,128)(2,1)}, u32[]{:S(2)}) %copy-start.1) | copy-done | bytes 56
  2.2 54.0 %layer.1 = (bf16[512,512]{1,0:T(8,128)(2,1)S(1)}, bf16[512,512]{1,0:T(8,128)(2,1)S(1)}, bf16[512,512]{1,0:T(8,128)(2,1)S(1)}, f32[512,128]{1,0:T(8,128)S(1)}, f32[4,4]{1,0:T(4,128)S(1)}) custom-call(bf16[512,512]{1,0:T(8,128)(2,1)} %q_hbm.1, bf16[512,512]{1,0:T(8,128)(2,1)} %k_hbm.1, bf16[512,512]{1,0:T(8,128)(2,1)} %v_hbm.1, bf16[512,4096]{1,0:T(8,128)(2,1)} %og_hbm.1, ...), custom_call_target="tpu_custom_call" | custom-call | flops 6400000000 | bytes 8000000 | tf_op jit(solution)/shard_map/layer/pallas_call | solution.py:631
  56.3 1.3 %results.1 = (bf16[512,512]{1,0:T(8,128)(2,1)}, bf16[512,512]{1,0:T(8,128)(2,1)}, bf16[512,512]{1,0:T(8,128)(2,1)}, f32[512,128]{1,0:T(8,128)}, f32[4,4]{1,0:T(4,128)}) custom-call(bf16[512,512]{1,0:T(8,128)(2,1)S(1)} %get-tuple-element.10.a, bf16[512,512]{1,0:T(8,128)(2,1)S(1)} %get-tuple-element.11.b, bf16[512,512]{1,0:T(8,128)(2,1)S(1)} %get-tuple-element.12.d, ...), custom_call_target="tpu_custom_call" | custom-call | tf_op jit(solution)/shard_map/results/pallas_call | solution.py:675
Async XLA Ops:
  0.6 0.9 %copy-start = (bf16[512,128]{1,0:T(8,128)(2,1)S(1)}, bf16[512,128]{1,0:T(8,128)(2,1)}, u32[]{:S(2)}) copy-start(bf16[512,128]{1,0:T(8,128)(2,1)} %w_hbm.1) | copy-start | bytes 393220
  1.5 0.7 %copy-start.1 = (bf16[4,4]{1,0:T(4,128)(2,1)S(1)}, bf16[4,4]{1,0:T(4,128)(2,1)}, u32[]{:S(2)}) copy-start(bf16[4,4]{1,0:T(4,128)(2,1)} %gain_ref.1) | copy-start | bytes 100

commit v4 on v3

--- a/solution.py
+++ b/solution.py
@@ -581,19 +581,21 @@
         gg_ref[:, j:j + 1] = jnp.sum(
             jnp.where(lane4 == 4 * s + j, gain_total, 0.0), axis=1, keepdims=True
         )
+    ag_drain()
+    scan_drain(0)
+    z_drain(0)
+    z_drain(1)
     scan_end(1)
     for h in range(NH):
         l = slice(h * HD, (h + 1) * HD)
         dk_o[:, l] = (dkp[:, l] + nt(v[:, l], st[1, l, :])).astype(BF)
+    dk_copy = pltpu.make_async_copy(dk_o, dk_hbm, out_sem.at[1])
+    dk_copy.start()
+    for h in range(NH):
+        l = slice(h * HD, (h + 1) * HD)
         dv_o[:, l] = (dvp[:, l] + nn(k[:, l], st[1, l, :])).astype(BF)
-    dk_copy = pltpu.make_async_copy(dk_o, dk_hbm, out_sem.at[1])
     dv_copy = pltpu.make_async_copy(dv_o, dv_hbm, out_sem.at[2])
-    dk_copy.start()
     dv_copy.start()
-    ag_drain()
-    scan_drain(0)
-    z_drain(0)
-    z_drain(1)
     rs_a_end(3)
     rs_b_end()
     wg_copy = pltpu.make_async_copy(wg_o, wg_hbm, out_sem.at[3])

time: 57.7 us -> 57.7 us (level)
  no operation moved by 1% of the time
where the time goes in v4:
time: 57.7 us; the launch traced here: 57.5 us
  Pallas kernels  55.3 us (96%)
  local copies, waits for them, and re-layouts  1.58 us (3%)
  between operations  0.65 us (1%)
    pallas_call x1, Pallas kernels, body(): pl.pallas_call(layer_kernel, out_shape=outs, in_specs=[hbm, hbm, hbm, hbm...  54 us
    unnamed x4, local copies, waits for them, and re-layouts  1.58 us
    pallas_call x1, Pallas kernels, body(): pl.pallas_call(copy_kernel, out_shape=outs, in_specs=[any_space] * 5, out...  1.27 us

profile of v4, /device:TPU:1, one launch (start us, length us, event | category | flops | bytes accessed | tf_op | source)
XLA Modules:
  0.0 57.5 jit_solution(9737927355904088422)
XLA Ops:
  0.6 0.0 copy-start
  0.6 0.9 %copy-done = bf16[512,128]{1,0:T(8,128)(2,1)S(1)} copy-done((bf16[512,128]{1,0:T(8,128)(2,1)S(1)}, bf16[512,128]{1,0:T(8,128)(2,1)}, u32[]{:S(2)}) %copy-start) | copy-done | bytes 131096
  1.5 0.0 copy-start.1
  1.5 0.7 %copy-done.1 = bf16[4,4]{1,0:T(4,128)(2,1)S(1)} copy-done((bf16[4,4]{1,0:T(4,128)(2,1)S(1)}, bf16[4,4]{1,0:T(4,128)(2,1)}, u32[]{:S(2)}) %copy-start.1) | copy-done | bytes 56
  2.2 54.0 %layer.1 = (bf16[512,512]{1,0:T(8,128)(2,1)S(1)}, bf16[512,512]{1,0:T(8,128)(2,1)S(1)}, bf16[512,512]{1,0:T(8,128)(2,1)S(1)}, f32[512,128]{1,0:T(8,128)S(1)}, f32[4,4]{1,0:T(4,128)S(1)}) custom-call(bf16[512,512]{1,0:T(8,128)(2,1)} %q_hbm.1, bf16[512,512]{1,0:T(8,128)(2,1)} %k_hbm.1, bf16[512,512]{1,0:T(8,128)(2,1)} %v_hbm.1, bf16[512,4096]{1,0:T(8,128)(2,1)} %og_hbm.1, ...), custom_call_target="tpu_custom_call" | custom-call | flops 6400000000 | bytes 8000000 | tf_op jit(solution)/shard_map/layer/pallas_call | solution.py:633
  56.3 1.3 %results.1 = (bf16[512,512]{1,0:T(8,128)(2,1)}, bf16[512,512]{1,0:T(8,128)(2,1)}, bf16[512,512]{1,0:T(8,128)(2,1)}, f32[512,128]{1,0:T(8,128)}, f32[4,4]{1,0:T(4,128)}) custom-call(bf16[512,512]{1,0:T(8,128)(2,1)S(1)} %get-tuple-element.10.a, bf16[512,512]{1,0:T(8,128)(2,1)S(1)} %get-tuple-element.11.b, bf16[512,512]{1,0:T(8,128)(2,1)S(1)} %get-tuple-element.12.d, ...), custom_call_target="tpu_custom_call" | custom-call | tf_op jit(solution)/shard_map/results/pallas_call | solution.py:677
Async XLA Ops:
  0.6 0.9 %copy-start = (bf16[512,128]{1,0:T(8,128)(2,1)S(1)}, bf16[512,128]{1,0:T(8,128)(2,1)}, u32[]{:S(2)}) copy-start(bf16[512,128]{1,0:T(8,128)(2,1)} %w_hbm.1) | copy-start | bytes 393220
  1.5 0.7 %copy-start.1 = (bf16[4,4]{1,0:T(4,128)(2,1)S(1)}, bf16[4,4]{1,0:T(4,128)(2,1)}, u32[]{:S(2)}) copy-start(bf16[4,4]{1,0:T(4,128)(2,1)} %gain_ref.1) | copy-start | bytes 100
